TPU v7x, 256 devices: a whole 4x4x8 slice. The times are simulated.
256 devices in a mesh: dom: 32 (over y, x, z_lo), cls: 8 (over z_hi, core).
Axes of the slice: x: 4, y: 4, z: 8 (z_hi: 4, z_lo: 2; z = z_hi * 2 + z_lo), core: 2. Of those that a mesh axis runs over, the one named last changes fastest.
Arguments:
- particles: bfloat16 [8192, 2, 4096], P(('dom', 'cls')), may hold values from -1200 to 1200
- defocus: bfloat16 [8192], P(('dom', 'cls')), may hold values from 1.2 to 3
- orient: int32 [8192, 16], P(('dom', 'cls')), may hold values from 0 to 47, as said below
- center: int32 [8192], P(('dom', 'cls')), may hold values from 0 to 48
- live: int32 [256], P(('dom', 'cls')), may hold values from 1 to 32, 4096 in all
- sigma2: float32 [4096], replicated, may hold values from 400 to 3000
- projections: bfloat16 [8, 48, 2, 4096], P('cls', None, None, 'dom'), may hold values from -5 to 5
Outputs:
- estimate: float32 [8, 48, 2, 4096], P('cls', None, None, 'dom')
- log_evidence: float32 [8192], P(('dom', 'cls'))
Inputs may be any that keep to these rules, and one draw needn't show every extreme that they name: `orient`: each row holds 16 different orientation indices. live particles fill the first slots of a device; some device is full.
All inputs are finite; a program needn't handle non-finite values.
Results may differ from a plain program's by a relative error of at most 0.003.
Values may be sent and summed in bfloat16 or wider, within the bound.
A program may use at most 256 MiB of HBM per device.

v0:
```python
import math

import jax
import jax.numpy as jnp
from jax import lax
from jax.experimental import pallas as pl
from jax.experimental.pallas import tpu as pltpu
from jax.sharding import PartitionSpec as P

FSIDE = 64
BOX = 128
GRID = 9
SHIFTS = 9
ORIENTS = 48
CANDS = 16
SLAB = 32

CTF_GAIN = 400.0
CTF_PHASE = 0.07
WIENER_TERM = 0.002

NX, NY, NH = 4, 4, 4
BLOCKS = 32
COLS = NH * ORIENTS
PAIR = 2 * SLAB
ROWS = 640
MESH = pl.DeviceIdType.MESH
F32, BF16 = jnp.float32, jnp.bfloat16

SIN_TERMS = (6.2831853025115025, -41.34170040531776, 81.60513138580835, -76.70301535406267,
             42.02592698764344, -14.899846674846755, 3.2381375198594955)
COS_TERMS = (0.9999999890590235, -19.73920449945402, 64.93911745989969, -85.45013953094733,
             60.16763095140483, -25.96759924996967, 6.5286581631738425)

AG_Z = 0
AG_2 = 3
AG_3 = 11
PART, PART_Z, PART_F = 35, 36, 37
AUX, AUX_Z, AUX_F = 38, 39, 40
SCORE, NORM, POST = 41, 42, 43
RS_1 = 44
RS_2 = 60
RS_Z = 72
COPIES = 78


def poly(terms, x):
    total = terms[-1] * x + terms[-2]
    for term in terms[-3::-1]:
        total = total * x + term
    return total


def sin_turns(t):
    return poly(SIN_TERMS, t * t) * t


def cos_turns(t):
    return poly(COS_TERMS, t * t)


def kernel(
    part_ref, orient_ref, center_ref, defocus_ref, live_ref, sigma_ref, proj_ref,
    est_ref, evid_ref,
    gath, imgs, aux, wide, tables, norm, shifted, ctf, corr, power_sum, expo, next_scores,
    few, few_in, few_post, few_post_in, post, post_z,
    acc, send1, recv1, send2, recv2, sums2, send3, recv3,
    send_sem, recv_sem, local_sem,
):
    dom, cls = lax.axis_index("dom"), lax.axis_index("cls")
    z_lo, x, y = lax.rem(dom, 2), lax.rem(dom // 2, 4), dom // 8
    core, z_hi = lax.rem(cls, 2), cls // 2
    z = z_hi * 2 + z_lo

    def device(yy, xx, zz):
        return ((yy * NX + xx) * 2 + lax.rem(zz, 2), (zz // 2) * 2 + core)

    def ring4(position, step):
        return lax.rem(position + step + 4, 4)

    def along(axis, step):
        if axis == 0:
            return device(y, ring4(x, step), z)
        return device(ring4(y, step), x, z)

    here = (x, y)
    partner = (dom, z_hi * 2 + 1 - core)
    beside = device(y, x, z_hi * 2 + 1 - z_lo)

    def along_z(step):
        return device(y, x, ring4(z_hi, step) * 2 + z_lo)

    def copy(index, source, target, to):
        return pltpu.make_async_remote_copy(
            src_ref=source, dst_ref=target, send_sem=send_sem.at[index],
            recv_sem=recv_sem.at[index], device_id=to, device_id_type=MESH,
        )

    pending = []

    def send(index, source, target, to):
        out = copy(index, source, target, to)
        out.start()
        pending.append(out)

    def arrived(index, target):
        copy(index, target, target, partner).wait_recv()

    barrier = pltpu.get_barrier_semaphore()
    friends = [partner, beside]
    friends += [along(axis, step) for axis in (0, 1) for step in (1, -1)]
    friends += [along_z(step) for step in range(1, NH)]
    for friend in friends:
        pl.semaphore_signal(barrier, inc=1, device_id=friend, device_id_type=MESH)

    own = [
        pltpu.make_async_copy(part_ref.at[z_lo], imgs.at[0, core], local_sem.at[0]),
        pltpu.make_async_copy(proj_ref, gath.at[y, x, z_hi], local_sem.at[1]),
    ]
    for item in own:
        item.start()
    pl.semaphore_wait(barrier, len(friends))

    mine = gath.at[y, x, z_hi]
    for step in range(1, NH):
        send(AG_Z + step - 1, proj_ref, mine, along_z(step))
    send(PART, part_ref.at[z_lo], imgs.at[0, core], partner)

    center = center_ref[...].astype(F32)
    center_y = jnp.floor((center + 0.5) * (1.0 / (GRID - 2)))
    center_x = center - center_y * (GRID - 2)
    slot = lax.broadcasted_iota(jnp.int32, (1, SLAB), 1)
    wide[...] = jnp.zeros_like(wide)
    wide[0:CANDS, 0:SLAB] = orient_ref[...].astype(F32)
    wide[16:17, 0:SLAB] = jnp.where(slot < live_ref[...], 1.0, 0.0)
    wide[17:18, 0:SLAB] = CTF_GAIN * defocus_ref[...].astype(F32)
    wide[18:19, 0:SLAB] = center_x + (1 - GRID // 2)
    wide[19:20, 0:SLAB] = center_y + (1 - GRID // 2)
    placed = pltpu.roll(wide[0:24, :], core * SLAB, 1)
    aux[0, core, 0:24, :] = placed + pltpu.roll(placed, 64, 1)
    aux[0, core, 24:56, :] = jnp.transpose(wide[...])[0:SLAB, :]
    send(AUX, aux.at[0, core], aux.at[0, core], partner)
    send(AUX_Z, aux.at[0, core], aux.at[1, core], beside)

    block_row = lax.broadcasted_iota(jnp.int32, (BLOCKS, 128), 0)
    lane = lax.broadcasted_iota(jnp.int32, (BLOCKS, 128), 1)
    v_all = (block_row * 2 + lane // FSIDE - FSIDE // 2).astype(F32)
    u_all = lax.rem(lane, FSIDE).astype(F32)
    tables[0] = (u_all * u_all + v_all * v_all) * (1.0 / (BOX * BOX))
    tables[1] = v_all
    tables[2] = cos_turns(v_all * (1.0 / BOX))
    tables[3] = sin_turns(v_all * (1.0 / BOX))
    tables[4] = 1.0 / sigma_ref[...]
    u = u_all[0:1, :]
    cos_u, sin_u = cos_turns(u * (1.0 / BOX)), sin_turns(u * (1.0 / BOX))
    for item in own:
        item.wait()

    def shift_tile(group, owner, tile):
        start = tile * 16
        info = aux[group, owner, 24 + start:40 + start, :]
        gain, t_x, t_y = info[:, 17:18], info[:, 18:19], info[:, 19:20]
        base_turn = u * t_x
        row0 = owner * SLAB + start

        def rows_at(base):
            return pl.ds(pl.multiple_of(base + row0, 16), 16)

        def step(at_yx, carry):
            d = at_yx * 2 + z_lo
            block = group * 16 + at_yx
            radius = tables[0, pl.ds(d, 1), :]
            v = tables[1, pl.ds(d, 1), :]
            cos_v = tables[2, pl.ds(d, 1), :]
            sin_v = tables[3, pl.ds(d, 1), :]
            inverse = tables[4, pl.ds(d, 1), :]
            lanes = pl.ds(pl.multiple_of(at_yx * 128, 128), 128)
            real = imgs[group, owner, 0, pl.ds(start, 16), lanes].astype(F32)
            imag = imgs[group, owner, 1, pl.ds(start, 16), lanes].astype(F32)
            angle = gain * radius + CTF_PHASE
            turns = jnp.floor(angle * (0.5 / math.pi) + 0.5)
            rest = (angle - turns * 6.28125) - turns * 0.0019353071795864769
            contrast = -sin_turns(rest * (0.5 / math.pi))
            weight = contrast * inverse
            ctf_weight = (contrast * contrast * inverse).astype(BF16)
            ctf[block, rows_at(PAIR), :] = ctf_weight
            turn = (base_turn + v * t_y) * (1.0 / BOX)
            turn = turn - jnp.floor(turn + 0.5)
            cosine, sine = cos_turns(turn), sin_turns(turn)
            real, imag = real * weight, imag * weight
            mid = (real * cosine - imag * sine, real * sine + imag * cosine)

            def rotations(value, cos_, sin_):
                re, im = value
                re_c, re_s, im_c, im_s = re * cos_, re * sin_, im * cos_, im * sin_
                return ((re_c + im_s, im_c - re_s), value, (re_c - im_s, im_c + re_s))

            for d_y, moved in enumerate(rotations(mid, cos_v, sin_v)):
                for d_x, (re, im) in enumerate(rotations(moved, cos_u, sin_u)):
                    at = rows_at((d_y * 3 + d_x) * PAIR)
                    shifted[block, at, 0:128] = re.astype(BF16)
                    shifted[block, at, 128:256] = im.astype(BF16)
            return carry

        lax.fori_loop(0, 16, step, 0, unroll=4)

    def zero_step(block, carry):
        shifted[block, SHIFTS * PAIR:, :] = jnp.zeros((ROWS - SHIFTS * PAIR, 256), BF16)
        ctf[block, 0:PAIR, :] = jnp.zeros((PAIR, 128), BF16)
        return carry

    def view(half, position, part=None):
        cut = pl.ds(half * 2, 2) if part is None else pl.ds(half * 2 + part, 1)
        if half == 0:
            return gath.at[y, position, cut]
        return gath.at[position, x, cut]

    def view_piece(half, piece, position):
        cut = pl.ds(half * 2, 2)
        if half == 0:
            return gath.at[position, ring4(x, piece), cut]
        return gath.at[ring4(y, piece), position, cut]

    def ring_first(half):
        ref = view(half, here[half])
        send(AG_2 + 4 * half, ref, ref, along(half, 1))
        send(AG_2 + 4 * half + 1, ref, ref, along(half, -1))

    def ring_second(half):
        base = AG_2 + 4 * half
        left, right = ring4(here[half], -1), ring4(here[half], 1)
        arrived(base, view(half, left))
        ref = view(half, left, 0)
        send(base + 2, ref, ref, along(half, 1))
        arrived(base + 1, view(half, right))
        ref = view(half, right, 1)
        send(base + 3, ref, ref, along(half, -1))

    def ring_end(half):
        far = ring4(here[half], 2)
        arrived(AG_2 + 4 * half + 2, view(half, far, 0))
        arrived(AG_2 + 4 * half + 3, view(half, far, 1))

    def piece_first(half, piece):
        axis = 1 - half
        base = AG_3 + 12 * half + 3 * piece
        ref = view_piece(half, piece, here[axis])
        send(base, ref, ref, along(axis, 1))
        send(base + 1, ref, ref, along(axis, -1))

    def piece_second(half, piece):
        axis = 1 - half
        base = AG_3 + 12 * half + 3 * piece
        left = view_piece(half, piece, ring4(here[axis], -1))
        right = view_piece(half, piece, ring4(here[axis], 1))
        if piece % 2 == 0:
            arrived(base, left)
            send(base + 2, left, left, along(axis, 1))
            arrived(base + 1, right)
        else:
            arrived(base + 1, right)
            send(base + 2, right, right, along(axis, -1))
            arrived(base, left)

    def piece_end(half, piece):
        axis = 1 - half
        far = view_piece(half, piece, ring4(here[axis], 2))
        arrived(AG_3 + 12 * half + 3 * piece + 2, far)

    contract_last = (((1,), (1,)), ((), ()))
    contract_plain = (((1,), (0,)), ((), ()))

    def score(blocks, kinds=(0, 1)):
        volumes = [gath[yy, xx].reshape(COLS, 256) for yy, xx in blocks]
        squares = []
        for volume in volumes:
            re, im = volume[:, 0:128].astype(F32), volume[:, 128:256].astype(F32)
            squares.append((re * re + im * im).astype(BF16))
        for kind in kinds:
            total = power = None
            for (yy, xx), volume, squared in zip(blocks, volumes, squares):
                block = kind * 16 + yy * 4 + xx
                term = lax.dot_general(
                    shifted[block], volume, contract_last, preferred_element_type=F32
                )
                term_p = lax.dot_general(
                    squared, ctf[block], contract_last, preferred_element_type=F32
                )
                total = term if total is None else total + term
                power = term_p if power is None else power + term_p
            corr[kind, :, 0:COLS] += total
            power_sum[kind] += power

    def near_step(k, carry):
        yy = ring4(y, k + k // 2)
        score([(yy, ring4(x, dx)) for dx in (0, 1, 3)])
        return carry

    def far_step(k, carry):
        step = k + k // 2
        score([(ring4(y, step), ring4(x, 2)), (ring4(y, 2), ring4(x, step))])
        return carry

    shift_tile(0, core, 0)
    shift_tile(0, core, 1)
    for step in range(1, NH):
        arrived(AG_Z + step - 1, gath.at[y, x, ring4(z_hi, -step)])
    for half in (0, 1):
        ring_first(half)
    for half in (0, 1):
        piece_first(half, 0)
    send(PART_Z, part_ref.at[1 - z_lo], imgs.at[1, core], beside)
    arrived(PART, imgs.at[0, 1 - core])
    arrived(AUX, aux.at[0, 1 - core])
    shift_tile(0, 1 - core, 0)
    for half in (0, 1):
        ring_second(half)
    for half in (0, 1):
        piece_first(half, 1)
        piece_first(half, 3)
    shift_tile(0, 1 - core, 1)
    for half in (0, 1):
        ring_end(half)
        piece_first(half, 2)
    for half in (0, 1):
        piece_second(half, 0)
    lax.fori_loop(0, 32, zero_step, 0)
    corr[...] = jnp.zeros_like(corr)
    power_sum[...] = jnp.zeros_like(power_sum)
    arrived(PART_Z, imgs.at[1, core])
    send(PART_F, imgs.at[1, core], imgs.at[1, core], partner)
    arrived(AUX_Z, aux.at[1, core])
    send(AUX_F, aux.at[1, core], aux.at[1, core], partner)
    shift_tile(1, core, 0)
    for half in (0, 1):
        piece_second(half, 1)
        piece_second(half, 3)
    shift_tile(1, core, 1)
    arrived(PART_F, imgs.at[1, 1 - core])
    arrived(AUX_F, aux.at[1, 1 - core])
    shift_tile(1, 1 - core, 0)
    for half in (0, 1):
        piece_second(half, 2)
    shift_tile(1, 1 - core, 1)
    lax.fori_loop(0, 3, near_step, 0)
    for half in (0, 1):
        for piece in (0, 1, 3):
            piece_end(half, piece)
    lax.fori_loop(0, 3, far_step, 0)
    for half in (0, 1):
        piece_end(half, 2)
    last = [(ring4(y, 2), ring4(x, 2))]
    score(last, (1,))

    def turn(kind, target):
        power_term = 0.5 * (power_sum[kind] + pltpu.roll(power_sum[kind], 64, 1))
        for tile in range(5):
            lanes = slice(tile * 128, tile * 128 + 128)
            target[:, lanes] = jnp.transpose(corr[kind, lanes, :])[0:COLS, :] - power_term

    row = lax.broadcasted_iota(jnp.int32, (ORIENTS, 128), 0).astype(F32)
    wide[32:56, :] = aux[1, 0, 0:24, :] + aux[1, 1, 0:24, :]
    turn(1, next_scores)

    def candidates(source, base):
        def few_step(j, carry):
            chosen = wide[pl.ds(base + j, 1), :] == row
            for h in range(NH):
                for tile in range(5):
                    part = source[h * ORIENTS:(h + 1) * ORIENTS, tile * 128:tile * 128 + 128]
                    value = jnp.sum(jnp.where(chosen, part, 0.0), axis=0, keepdims=True)
                    few[h * 5 + tile, pl.ds(j, 1), :] = value
            return carry

        lax.fori_loop(0, CANDS, few_step, 0)

    candidates(next_scores, 32)
    score_sent = copy(SCORE, few, few_in, beside)
    score_sent.start()
    score(last, (0,))
    turn(0, expo)

    info = aux[0, 0, 0:24, :] + aux[0, 1, 0:24, :]
    wide[64:88, :] = info
    allowed = jnp.zeros((ORIENTS, 128), jnp.bool_)
    for j in range(CANDS):
        allowed = allowed | (info[j:j + 1, :] == row)
    allowed = jnp.where(allowed, 1.0, 0.0)
    allowed = jnp.concatenate([allowed] * NH, axis=0) > 0.5
    lower = lax.broadcasted_iota(jnp.int32, (COLS, 128), 1) < PAIR
    live = info[CANDS:CANDS + 1, :]
    least = jnp.float32(-3.0e38)
    arrived(SCORE, few_in)

    def spread(h, source, base):
        added = [jnp.zeros((ORIENTS, 128), F32) for _ in range(5)]
        for j in range(CANDS):
            chosen = wide[base + j:base + j + 1, :] == row
            for tile in range(5):
                value = source[h * 5 + tile, j:j + 1, :]
                added[tile] = jnp.where(chosen, value, added[tile])
        return added

    def class_rows(h):
        return pl.ds(pl.multiple_of(h * ORIENTS, 16), ORIENTS)

    def spread_step(h, carry):
        for tile, added in enumerate(spread(h, few_in, 64)):
            expo[class_rows(h), tile * 128:tile * 128 + 128] += added
        return carry

    lax.fori_loop(0, NH, spread_step, 0)
    highest = jnp.full((1, 128), least, F32)
    for tile in range(5):
        lanes = slice(tile * 128, tile * 128 + 128)
        valid = allowed & lower if tile == 4 else allowed
        scores = jnp.where(valid, expo[:, lanes], least)
        highest = jnp.maximum(highest, jnp.max(scores, axis=0, keepdims=True))
    highest = jnp.maximum(highest, pltpu.roll(highest, 64, 1))
    partition = jnp.zeros((1, 128), F32)
    for tile in range(5):
        lanes = slice(tile * 128, tile * 128 + 128)
        valid = allowed & lower if tile == 4 else allowed
        terms = jnp.where(valid, jnp.exp(expo[:, lanes] - highest), 0.0)
        expo[:, lanes] = terms
        partition = partition + jnp.sum(terms, axis=0, keepdims=True)
    partition = partition + pltpu.roll(partition, 64, 1)

    norm[core, 0:1, :] = highest
    norm[core, 1:2, :] = partition
    norm[core, 2:8, :] = jnp.zeros((6, 128), F32)
    send(NORM, norm.at[core], norm.at[core], partner)
    arrived(NORM, norm.at[1 - core])
    other = norm[1 - core]
    peak = jnp.maximum(highest, other[0:1, :])
    mine_scale = jnp.exp(highest - peak)
    whole = partition * mine_scale + other[1:2, :] * jnp.exp(other[0:1, :] - peak)
    scale = jnp.where(live > 0.5, mine_scale / whole, 0.0)
    mass = jnp.zeros((COLS, 128), F32)
    for tile in range(5):
        lanes = slice(tile * 128, tile * 128 + 128)
        posterior = (expo[:, lanes] * scale).astype(BF16).astype(F32)
        mass = mass + posterior
        expo[:, lanes] = posterior
        if tile == 4:
            mass = mass + pltpu.roll(mass, 64, 1)
            posterior = jnp.where(lower, posterior, mass)
        post[:, lanes] = posterior.astype(BF16)
    score_sent.wait_send()
    candidates(expo, 64)
    few_post[...] = few[...].astype(BF16)
    send(POST, few_post, few_post_in, beside)
    evidence = jnp.where(live > 0.5, peak + jnp.log(whole), 0.0)
    evidence = pltpu.roll(jnp.broadcast_to(evidence, evid_ref.shape), lax.rem(128 - core * SLAB, 128), 1)
    evid_ref[...] = evidence

    def project(weights, block):
        data = lax.dot_general(
            weights[...], shifted[block], contract_plain, preferred_element_type=F32
        )
        weight = lax.dot_general(
            weights[:, 512:640], ctf[block], contract_plain, preferred_element_type=F32
        )
        return data, weight

    def place(r):
        return ring4(y, r // 4) * 4 + ring4(x, lax.rem(r, 4))

    def own_step(r, carry):
        data, weight = project(post, place(r))
        acc[r, :, 0:256] = data
        acc[r, :, 256:384] = weight
        return carry

    def next_step(r):
        data, weight = project(post_z, 16 + place(r))
        acc[r, :, 0:256] += data
        acc[r, :, 256:384] += weight

    lax.fori_loop(0, 16, own_step, 0)
    arrived(POST, few_post_in)
    few_in[...] = few_post_in[...].astype(F32)
    lower_part = lax.broadcasted_iota(jnp.int32, (ORIENTS, 128), 1) < PAIR

    def spread_post(h, carry):
        mass = jnp.zeros((ORIENTS, 128), F32)
        for tile, value in enumerate(spread(h, few_in, 32)):
            mass = mass + value
            if tile == 4:
                mass = mass + pltpu.roll(mass, 64, 1)
                value = jnp.where(lower_part, value, mass)
            post_z[class_rows(h), tile * 128:tile * 128 + 128] = value.astype(BF16)
        return carry

    lax.fori_loop(0, NH, spread_post, 0)

    edge = COLS // 2

    def pack(half, slot, i, target, other, added=None):
        rows = slice(half * edge, half * edge + edge)
        value = acc[other * 4 + target if half == 0 else target * 4 + other, rows, :]
        if added is not None:
            value = value + recv1[half, added, i].astype(F32)
        send1[half, slot, i] = value.astype(BF16)

    def piece(half, slot, target, first):
        for i in (0, 1):
            pack(half, slot, i, target, first + i)
        send(
            RS_1 + 8 * half + slot, send1.at[half, slot], recv1.at[half, slot],
            along(half, 1 if slot % 2 == 0 else -1),
        )

    def piece_sum(half, slot, i, target, other, added):
        pack(half, slot, i, target, other, added)
        send(
            RS_1 + 8 * half + 2 * slot - 4 + i, send1.at[half, slot, i], recv1.at[half, slot, i],
            along(half, 1 if slot % 2 == 0 else -1),
        )

    def loop(count, index):
        def step(k, carry):
            next_step(index(k))
            return carry

        lax.fori_loop(0, count, step, 0)

    loop(4, lambda k: k * 4 + 2)
    piece(0, 0, 2, 0)
    piece(0, 1, 2, 2)
    loop(3, lambda k: 8 + k + k // 2)
    piece(1, 0, 2, 0)
    piece(1, 1, 2, 2)
    loop(9, lambda k: (k // 3 + k // 6) * 4 + lax.rem(k, 3) + lax.rem(k, 3) // 2)
    for half in (0, 1):
        piece(half, 2, 1, 2)
        piece(half, 3, 3, 0)
    for half in (0, 1):
        arrived(RS_1 + 8 * half + 1, recv1.at[half, 1])
        piece_sum(half, 5, 0, 3, 2, 1)
        arrived(RS_1 + 8 * half, recv1.at[half, 0])
        piece_sum(half, 4, 1, 1, 1, 0)
    for half in (0, 1):
        piece_sum(half, 5, 1, 3, 3, 1)
        piece_sum(half, 4, 0, 1, 0, 0)

    def relay_rows(half, top):
        start = half * edge + top * ORIENTS
        return slice(start, start + ORIENTS)

    def relay(half, slot, distance, top, added=None):
        r = distance * 4 if half == 0 else distance
        value = acc[r, relay_rows(half, top), :]
        if added is not None:
            arrived(RS_2 + 6 * half + added, recv2.at[half, added])
            value = value + recv2[half, added]
        send2[half, slot] = value
        send(
            RS_2 + 6 * half + slot, send2.at[half, slot], recv2.at[half, slot],
            along(1 - half, 1 if slot % 2 == 0 else -1),
        )

    for other in (2, 1, 3, 0):
        i = other % 2
        whole_slot, split_slot = (3, 4) if other < 2 else (2, 5)
        for half in (0, 1):
            rows = slice(half * edge, half * edge + edge)
            if other in (1, 2):
                arrived(RS_1 + 8 * half + whole_slot, recv1.at[half, whole_slot])
            arrived(RS_1 + 8 * half + 2 * split_slot - 4 + i, recv1.at[half, split_slot, i])
            r = other * 4 if half == 0 else other
            acc[r, rows, :] += (
                recv1[half, whole_slot, i].astype(F32) + recv1[half, split_slot, i].astype(F32)
            )
            if other == 2:
                relay(half, 0, 2, 0)
                relay(half, 1, 2, 1)
            elif other == 1:
                relay(half, 2, 1, 1)
            elif other == 3:
                relay(half, 3, 3, 0)
    for half in (0, 1):
        relay(half, 4, 1, 0, 0)
        relay(half, 5, 3, 1, 1)

    for half in (0, 1):
        for slot in range(2, 6):
            arrived(RS_2 + 6 * half + slot, recv2.at[half, slot])
        sums2[half * 2] = acc[0, relay_rows(half, 0), :] + recv2[half, 3] + recv2[half, 4]
        sums2[half * 2 + 1] = acc[0, relay_rows(half, 1), :] + recv2[half, 2] + recv2[half, 5]

    middle = ORIENTS // 2

    def pass_on(slot, distance, top, added=None):
        value = sums2[ring4(z_hi, distance), top * middle:(top + 1) * middle, :]
        if added is not None:
            arrived(RS_Z + added, recv3.at[added])
            value = value + recv3[added]
        send3[slot] = value
        to = along_z(1 if slot % 2 == 0 else -1)
        send(RS_Z + slot, send3.at[slot], recv3.at[slot], to)

    pass_on(0, 2, 0)
    pass_on(1, 2, 1)
    pass_on(2, 1, 1)
    pass_on(3, -1, 0)
    pass_on(4, 1, 0, 0)
    pass_on(5, -1, 1, 1)
    for slot in range(2, 6):
        arrived(RS_Z + slot, recv3.at[slot])
    for top in (0, 1):
        rows = slice(top * middle, (top + 1) * middle)
        near, far = ((3, 4), (2, 5))[top]
        total = sums2[z_hi, rows, :] + recv3[near] + recv3[far]
        divisor = total[:, 256:384] + WIENER_TERM
        est_ref[rows, 0:128] = total[:, 0:128] / divisor
        est_ref[rows, 128:256] = total[:, 128:256] / divisor

    for item in pending:
        item.wait_send()


def on_device(particles, defocus, orient, center, live, sigma2, projections):
    images = particles.reshape(SLAB, 2, 16, 2, 128).transpose(3, 1, 0, 2, 4).reshape(2, 2, SLAB, 2048)
    vmem = pl.BlockSpec(memory_space=pltpu.VMEM)
    estimate, evidence = pl.pallas_call(
        kernel,
        out_shape=(
            jax.ShapeDtypeStruct((ORIENTS, 256), F32),
            jax.ShapeDtypeStruct((8, 128), F32),
        ),
        in_specs=[vmem] * 7,
        out_specs=(vmem, vmem),
        scratch_shapes=[
            pltpu.VMEM((NY, NX, NH, ORIENTS, 256), BF16),
            pltpu.VMEM((2, 2, 2, SLAB, 2048), BF16),
            pltpu.VMEM((2, 2, 56, 128), F32),
            pltpu.VMEM((128, 128), F32),
            pltpu.VMEM((5, BLOCKS, 128), F32),
            pltpu.VMEM((2, 8, 128), F32),
            pltpu.VMEM((32, ROWS, 256), BF16),
            pltpu.VMEM((32, 128, 128), BF16),
            pltpu.VMEM((2, ROWS, 256), F32),
            pltpu.VMEM((2, COLS, 128), F32),
            pltpu.VMEM((COLS, ROWS), F32),
            pltpu.VMEM((COLS, ROWS), F32),
            pltpu.VMEM((5 * NH, CANDS, 128), F32),
            pltpu.VMEM((5 * NH, CANDS, 128), F32),
            pltpu.VMEM((5 * NH, CANDS, 128), BF16),
            pltpu.VMEM((5 * NH, CANDS, 128), BF16),
            pltpu.VMEM((COLS, ROWS), BF16),
            pltpu.VMEM((COLS, ROWS), BF16),
            pltpu.VMEM((16, COLS, 384), F32),
            pltpu.VMEM((2, 6, 2, COLS // 2, 384), BF16),
            pltpu.VMEM((2, 6, 2, COLS // 2, 384), BF16),
            pltpu.VMEM((2, 6, ORIENTS, 384), F32),
            pltpu.VMEM((2, 6, ORIENTS, 384), F32),
            pltpu.VMEM((NH, ORIENTS, 384), F32),
            pltpu.VMEM((6, ORIENTS // 2, 384), F32),
            pltpu.VMEM((6, ORIENTS // 2, 384), F32),
            pltpu.SemaphoreType.DMA((COPIES,)),
            pltpu.SemaphoreType.DMA((COPIES,)),
            pltpu.SemaphoreType.DMA((2,)),
        ],
        compiler_params=pltpu.CompilerParams(
            collective_id=0, has_side_effects=True, vmem_limit_bytes=50 * 1024 * 1024
        ),
    )(
        images, orient.T, center.reshape(1, SLAB), defocus.reshape(1, SLAB), live.reshape(1, 1),
        sigma2.reshape(BLOCKS, 128), projections.reshape(ORIENTS, 256),
    )
    return (estimate.reshape(1, ORIENTS, 2, 128), evidence[0, 0:SLAB])


def solution(mesh):
    return jax.shard_map(
        on_device,
        mesh=mesh,
        in_specs=(
            P(("dom", "cls"), None, None),
            P(("dom", "cls")),
            P(("dom", "cls"), None),
            P(("dom", "cls")),
            P(("dom", "cls")),
            P(),
            P("cls", None, None, "dom"),
        ),
        out_specs=(P("cls", None, None, "dom"), P(("dom", "cls"))),
        check_vma=False,
    )
```

profile of v0, /device:TPU:1, one launch (start us, length us, event | category | flops | bytes accessed | tf_op | source)
XLA Modules:
  0.0 80.9 jit_solution(13035079228858304844)
XLA Ops:
  0.6 1.4 %reshape.28 = bf16[32,2,16,2,128]{4,3,2,1,0:T(2,128)(2,1)S(1)} reshape(bf16[32,2,4096]{2,1,0:T(2,128)(2,1)} %param.7) | data formatting | bytes 1048576 | tf_op jit(solution)/shard_map/reshape | solution.py:624
  2.1 0.1 copy.13
  2.1 0.0 copy-start.4
  2.2 0.2 reshape.29.part_ref
  2.4 0.5 copy-done.4
  2.9 0.0 copy-start
  2.9 0.0 copy-start.1
  3.6 0.0 copy-start.2
  3.6 0.0 copy-start.3
  3.6 0.0 copy-done
  3.6 0.0 copy-done.1
  3.6 0.6 copy-done.2
  4.2 0.0 copy-done.3
  4.2 75.5 %shard_map.86 = (f32[48,256]{1,0:T(8,128)S(1)}, f32[8,128]{1,0:T(8,128)S(1)}) custom-call(bf16[2,2,32,2048]{3,2,1,0:T(8,128)(2,1)S(1)} %reshape.29.part_ref, s32[16,32]{1,0:T(8,128)S(1)} %bitcast.20, s32[1,32]{1,0:T(1,128)S(1)} %bitcast.21, bf16[1,32]{1,0:T(2,128)(2,1)S(1)} %bitcast.22, s32[1,1]{1,0:T(1,128)} %bitcast.17.live_ref, f32[32,128]{1,0:T(8,128)S(1)} %bitcast.19, ...), custom_call_target="tpu_custom_call" | custom-call | tf_op jit(solution)/shard_map/pallas_call | solution.py:626
  79.8 0.6 reshape.35
  80.4 0.5 slice_bitcast_fusion
  (1 shorter events, 0.0 us)
Async XLA Ops:
  2.1 0.7 copy-start.4
  2.9 0.7 copy-start
  2.9 0.7 copy-start.1
  3.6 0.7 copy-start.2
  3.6 0.7 copy-start.3
where the time goes:
time: 81.2 us; the launch traced here: 80.9 us
  Pallas kernels  75.5 us (93%)
  local copies, waits for them, and re-layouts  4.05 us (5%)
  between operations  1.36 us (2%)
    pallas_call x1, Pallas kernels, on_device(): pl.pallas_call(kernel, out_shape=(jax.ShapeDtypeStruct((ORIENTS, 256), F3...  75.5 us
    reshape x3, local copies, waits for them, and re-layouts, on_device(): particles.reshape(SLAB, 2, 16, 2, 128).transpose(3, 1, 0, 2, 4)  1.73 us

commit v1 on v0

--- a/solution.py
+++ b/solution.py
@@ -41,7 +41,8 @@
 RS_1 = 44
 RS_2 = 60
 RS_Z = 72
-COPIES = 78
+SCORE_2 = 78
+COPIES = 79
 
 
 def poly(terms, x):
@@ -327,20 +328,20 @@
     lax.fori_loop(0, 32, zero_step, 0)
     corr[...] = jnp.zeros_like(corr)
     power_sum[...] = jnp.zeros_like(power_sum)
+    for half in (0, 1):
+        piece_second(half, 1)
+        piece_second(half, 3)
     arrived(PART_Z, imgs.at[1, core])
     send(PART_F, imgs.at[1, core], imgs.at[1, core], partner)
     arrived(AUX_Z, aux.at[1, core])
     send(AUX_F, aux.at[1, core], aux.at[1, core], partner)
     shift_tile(1, core, 0)
     for half in (0, 1):
-        piece_second(half, 1)
-        piece_second(half, 3)
+        piece_second(half, 2)
     shift_tile(1, core, 1)
     arrived(PART_F, imgs.at[1, 1 - core])
     arrived(AUX_F, aux.at[1, 1 - core])
     shift_tile(1, 1 - core, 0)
-    for half in (0, 1):
-        piece_second(half, 2)
     shift_tile(1, 1 - core, 1)
     lax.fori_loop(0, 3, near_step, 0)
     for half in (0, 1):
@@ -362,7 +363,7 @@
     wide[32:56, :] = aux[1, 0, 0:24, :] + aux[1, 1, 0:24, :]
     turn(1, next_scores)
 
-    def candidates(source, base):
+    def candidates(source, base, first, last):
         def few_step(j, carry):
             chosen = wide[pl.ds(base + j, 1), :] == row
             for h in range(NH):
@@ -372,11 +373,14 @@
                     few[h * 5 + tile, pl.ds(j, 1), :] = value
             return carry
 
-        lax.fori_loop(0, CANDS, few_step, 0)
-
-    candidates(next_scores, 32)
-    score_sent = copy(SCORE, few, few_in, beside)
-    score_sent.start()
+        lax.fori_loop(first, last, few_step, 0)
+
+    sent = []
+    for part, index in ((0, SCORE), (1, SCORE_2)):
+        candidates(next_scores, 32, part * 8, part * 8 + 8)
+        cut = pl.ds(part * 8, 8)
+        sent.append(copy(index, few.at[:, cut, :], few_in.at[:, cut, :], beside))
+        sent[-1].start()
     score(last, (0,))
     turn(0, expo)
 
@@ -390,7 +394,8 @@
     lower = lax.broadcasted_iota(jnp.int32, (COLS, 128), 1) < PAIR
     live = info[CANDS:CANDS + 1, :]
     least = jnp.float32(-3.0e38)
-    arrived(SCORE, few_in)
+    arrived(SCORE, few_in.at[:, pl.ds(0, 8), :])
+    arrived(SCORE_2, few_in.at[:, pl.ds(8, 8), :])
 
     def spread(h, source, base):
         added = [jnp.zeros((ORIENTS, 128), F32) for _ in range(5)]
@@ -446,8 +451,9 @@
             mass = mass + pltpu.roll(mass, 64, 1)
             posterior = jnp.where(lower, posterior, mass)
         post[:, lanes] = posterior.astype(BF16)
-    score_sent.wait_send()
-    candidates(expo, 64)
+    for item in sent:
+        item.wait_send()
+    candidates(expo, 64, 0, CANDS)
     few_post[...] = few[...].astype(BF16)
     send(POST, few_post, few_post_in, beside)
     evidence = jnp.where(live > 0.5, peak + jnp.log(whole), 0.0)
@@ -560,7 +566,7 @@
             along(1 - half, 1 if slot % 2 == 0 else -1),
         )
 
-    for other in (2, 1, 3, 0):
+    def first_sum(other):
         i = other % 2
         whole_slot, split_slot = (3, 4) if other < 2 else (2, 5)
         for half in (0, 1):
@@ -579,9 +585,13 @@
                 relay(half, 2, 1, 1)
             elif other == 3:
                 relay(half, 3, 3, 0)
+
+    for other in (2, 1, 3):
+        first_sum(other)
     for half in (0, 1):
         relay(half, 4, 1, 0, 0)
         relay(half, 5, 3, 1, 1)
+    first_sum(0)
 
     for half in (0, 1):
         for slot in range(2, 6):

time: 81.2 us -> 82.4 us (1.015)
  Pallas kernels: 75.5 us -> 76.5 us
    pallas_call x1, Pallas kernels: 75.5 us -> 76.5 us  [on_device(): pl.pallas_call(kernel, out_shape=(jax.ShapeDtypeStruct((ORIENTS, 256), F3...]
where the time goes in v1:
time: 82.4 us; the launch traced here: 82 us
  Pallas kernels  76.5 us (93%)
  local copies, waits for them, and re-layouts  4.05 us (5%)
  between operations  1.36 us (2%)
    pallas_call x1, Pallas kernels, on_device(): pl.pallas_call(kernel, out_shape=(jax.ShapeDtypeStruct((ORIENTS, 256), F3...  76.5 us
    reshape x3, local copies, waits for them, and re-layouts, on_device(): particles.reshape(SLAB, 2, 16, 2, 128).transpose(3, 1, 0, 2, 4)  1.73 us

profile of v1, /device:TPU:1, one launch (start us, length us, event | category | flops | bytes accessed | tf_op | source)
XLA Modules:
  0.0 82.0 jit_solution(11229757887977030666)
XLA Ops:
  0.6 1.4 %reshape.28 = bf16[32,2,16,2,128]{4,3,2,1,0:T(2,128)(2,1)S(1)} reshape(bf16[32,2,4096]{2,1,0:T(2,128)(2,1)} %param.7) | data formatting | bytes 1048576 | tf_op jit(solution)/shard_map/reshape | solution.py:634
  2.1 0.1 copy.13
  2.1 0.0 copy-start.4
  2.2 0.2 reshape.29.part_ref
  2.4 0.5 copy-done.4
  2.9 0.0 copy-start
  2.9 0.0 copy-start.1
  3.6 0.0 copy-start.2
  3.6 0.0 copy-start.3
  3.6 0.0 copy-done
  3.6 0.0 copy-done.1
  3.6 0.6 copy-done.2
  4.2 0.0 copy-done.3
  4.2 76.5 %shard_map.86 = (f32[48,256]{1,0:T(8,128)S(1)}, f32[8,128]{1,0:T(8,128)S(1)}) custom-call(bf16[2,2,32,2048]{3,2,1,0:T(8,128)(2,1)S(1)} %reshape.29.part_ref, s32[16,32]{1,0:T(8,128)S(1)} %bitcast.20, s32[1,32]{1,0:T(1,128)S(1)} %bitcast.21, bf16[1,32]{1,0:T(2,128)(2,1)S(1)} %bitcast.22, s32[1,1]{1,0:T(1,128)} %bitcast.17.live_ref, f32[32,128]{1,0:T(8,128)S(1)} %bitcast.19, ...), custom_call_target="tpu_custom_call" | custom-call | tf_op jit(solution)/shard_map/pallas_call | solution.py:636
  80.8 0.6 reshape.35
  81.5 0.5 slice_bitcast_fusion
  (1 shorter events, 0.0 us)
Async XLA Ops:
  2.1 0.7 copy-start.4
  2.9 0.7 copy-start
  2.9 0.7 copy-start.1
  3.6 0.7 copy-start.2
  3.6 0.7 copy-start.3

commit v2 on v0

--- a/solution.py
+++ b/solution.py
@@ -202,7 +202,7 @@
                     shifted[block, at, 128:256] = im.astype(BF16)
             return carry
 
-        lax.fori_loop(0, 16, step, 0, unroll=4)
+        lax.fori_loop(0, 16, step, 0, unroll=8)
 
     def zero_step(block, carry):
         shifted[block, SHIFTS * PAIR:, :] = jnp.zeros((ROWS - SHIFTS * PAIR, 256), BF16)
@@ -303,6 +303,9 @@
 
     shift_tile(0, core, 0)
     shift_tile(0, core, 1)
+    lax.fori_loop(0, 32, zero_step, 0)
+    corr[...] = jnp.zeros_like(corr)
+    power_sum[...] = jnp.zeros_like(power_sum)
     for step in range(1, NH):
         arrived(AG_Z + step - 1, gath.at[y, x, ring4(z_hi, -step)])
     for half in (0, 1):
@@ -324,9 +327,6 @@
         piece_first(half, 2)
     for half in (0, 1):
         piece_second(half, 0)
-    lax.fori_loop(0, 32, zero_step, 0)
-    corr[...] = jnp.zeros_like(corr)
-    power_sum[...] = jnp.zeros_like(power_sum)
     arrived(PART_Z, imgs.at[1, core])
     send(PART_F, imgs.at[1, core], imgs.at[1, core], partner)
     arrived(AUX_Z, aux.at[1, core])
@@ -560,7 +560,7 @@
             along(1 - half, 1 if slot % 2 == 0 else -1),
         )
 
-    for other in (2, 1, 3, 0):
+    def first_sum(other):
         i = other % 2
         whole_slot, split_slot = (3, 4) if other < 2 else (2, 5)
         for half in (0, 1):
@@ -579,9 +579,13 @@
                 relay(half, 2, 1, 1)
             elif other == 3:
                 relay(half, 3, 3, 0)
+
+    for other in (2, 1, 3):
+        first_sum(other)
     for half in (0, 1):
         relay(half, 4, 1, 0, 0)
         relay(half, 5, 3, 1, 1)
+    first_sum(0)
 
     for half in (0, 1):
         for slot in range(2, 6):

time: 81.2 us -> 81 us (level)
  no operation moved by 1% of the time
where the time goes in v2:
time: 81 us; the launch traced here: 80.7 us
  Pallas kernels  75.3 us (93%)
  local copies, waits for them, and re-layouts  4.05 us (5%)
  between operations  1.36 us (2%)
    pallas_call x1, Pallas kernels, on_device(): pl.pallas_call(kernel, out_shape=(jax.ShapeDtypeStruct((ORIENTS, 256), F3...  75.3 us
    reshape x3, local copies, waits for them, and re-layouts, on_device(): particles.reshape(SLAB, 2, 16, 2, 128).transpose(3, 1, 0, 2, 4)  1.73 us

profile of v2, /device:TPU:1, one launch (start us, length us, event | category | flops | bytes accessed | tf_op | source)
XLA Modules:
  0.0 80.7 jit_solution(17110179264447686541)
XLA Ops:
  0.6 1.4 %reshape.28 = bf16[32,2,16,2,128]{4,3,2,1,0:T(2,128)(2,1)S(1)} reshape(bf16[32,2,4096]{2,1,0:T(2,128)(2,1)} %param.7) | data formatting | bytes 1048576 | tf_op jit(solution)/shard_map/reshape | solution.py:628
  2.1 0.1 copy.13
  2.1 0.0 copy-start.4
  2.2 0.2 reshape.29.part_ref
  2.4 0.5 copy-done.4
  2.9 0.0 copy-start
  2.9 0.0 copy-start.1
  3.6 0.0 copy-start.2
  3.6 0.0 copy-start.3
  3.6 0.0 copy-done
  3.6 0.0 copy-done.1
  3.6 0.6 copy-done.2
  4.2 0.0 copy-done.3
  4.2 75.3 %shard_map.86 = (f32[48,256]{1,0:T(8,128)S(1)}, f32[8,128]{1,0:T(8,128)S(1)}) custom-call(bf16[2,2,32,2048]{3,2,1,0:T(8,128)(2,1)S(1)} %reshape.29.part_ref, s32[16,32]{1,0:T(8,128)S(1)} %bitcast.20, s32[1,32]{1,0:T(1,128)S(1)} %bitcast.21, bf16[1,32]{1,0:T(2,128)(2,1)S(1)} %bitcast.22, s32[1,1]{1,0:T(1,128)} %bitcast.17.live_ref, f32[32,128]{1,0:T(8,128)S(1)} %bitcast.19, ...), custom_call_target="tpu_custom_call" | custom-call | tf_op jit(solution)/shard_map/pallas_call | solution.py:630
  79.6 0.6 reshape.35
  80.2 0.5 slice_bitcast_fusion
  (1 shorter events, 0.0 us)
Async XLA Ops:
  2.1 0.7 copy-start.4
  2.9 0.7 copy-start
  2.9 0.7 copy-start.1
  3.6 0.7 copy-start.2
  3.6 0.7 copy-start.3
